TPU v7x, 256 devices: a whole 4x4x8 slice. The times are simulated.
256 devices in a mesh: row: 32 (over x_hi, z, core), col: 8 (over y, x_lo).
Axes of the slice: x: 4 (x_hi: 2, x_lo: 2; x = x_hi * 2 + x_lo), y: 4, z: 8, core: 2. Of those that a mesh axis runs over, the one named last changes fastest.
Arguments:
- out_grad: bfloat16 [1792, 16384], P('row', 'col'), may hold values from -0.8984375 to 0.8984375
- gate_pre: bfloat16 [1792, 28672], P('col', 'row'), may hold values from -9 to 9
- up_pre: bfloat16 [1792, 28672], P('col', 'row'), may hold values from -0.8984375 to 0.8984375
- w_down: bfloat16 [28672, 16384], P('row', 'col'), may hold values from -0.046875 to 0.046875
Outputs:
- grad_down: bfloat16 [28672, 16384], P('row', 'col')
- grad_gate: bfloat16 [1792, 28672], P('col', 'row')
- grad_up: bfloat16 [1792, 28672], P('col', 'row')
All inputs are finite; a program needn't handle non-finite values.
Results may differ from a plain program's by a relative error of at most 0.0049.
Values may be sent and summed in bfloat16 or wider, within the bound.
A program may use at most 128 MiB of HBM per device.

v0:
```python
import jax
import jax.numpy as jnp
from jax import lax
from jax.sharding import PartitionSpec as P


def times_weight(panel, weight):
    return lax.dot_general(
        panel, weight, (((1,), (1,)), ((), ())), preferred_element_type=jnp.float32
    )


def token_contract(left, right):
    return lax.dot_general(
        left, right, (((0,), (0,)), ((), ())), preferred_element_type=jnp.float32
    )


def swiglu_parts(hidden_grad, gate_pre, up_pre):
    gate = gate_pre.astype(jnp.float32)
    upper = up_pre.astype(jnp.float32)
    sig = jax.nn.sigmoid(gate)
    silu = gate * sig
    hidden = (silu * upper).astype(jnp.bfloat16)
    grad_up = (hidden_grad * silu).astype(jnp.bfloat16)
    grad_gate = (hidden_grad * upper * sig * (1.0 + gate * (1.0 - sig))).astype(jnp.bfloat16)
    return (hidden, grad_gate, grad_up)


def on_device(out_grad, gate_pre, up_pre, w_down):
    panel = lax.all_gather(out_grad, "row", axis=0, tiled=True)
    own_grad = lax.psum_scatter(times_weight(panel, w_down), "col", scatter_dimension=0, tiled=True)
    hidden, grad_gate, grad_up = swiglu_parts(own_grad, gate_pre, up_pre)
    hidden_all = lax.all_gather(hidden, "col", axis=0, tiled=True)
    grad_down = token_contract(hidden_all, panel).astype(jnp.bfloat16)
    return (grad_down, grad_gate, grad_up)


def solution(mesh):
    return jax.shard_map(
        on_device,
        mesh=mesh,
        in_specs=(P("row", "col"), P("col", "row"), P("col", "row"), P("row", "col")),
        out_specs=(P("row", "col"), P("col", "row"), P("col", "row")),
        check_vma=False,
    )
```

profile of v0, /device:TPU:40, one launch (start us, length us, event | category | flops | bytes accessed | tf_op | source)
XLA Modules:
  0.0 351.1 jit_solution(12279129825678741531)
XLA Ops:
  7.2 0.0 all-gather.5.cloned.1.call-start
  7.2 0.7 all-gather.5.cloned.1.call-update
  7.9 0.0 reduce-scatter.2.cloned.1.call-start
  7.9 102.9 %all-gather.5.cloned.1.call-done = bf16[1792,2048]{1,0:T(8,128)(2,1)} async-done(((bf16[56,2048]{1,0:T(8,128)(2,1)}), bf16[1792,2048]{1,0:T(8,128)(2,1)}) %all-gather.5.cloned.1.call-update) | async-done | bytes 7340048 | tf_op jit(solution)/shard_map/all_gather | solution.py:31
  110.9 12.9 %fusion.8 = f32[1792,896]{1,0:T(8,128)} fusion(bf16[1792,2048]{1,0:T(8,128)(2,1)} %all-gather.5.cloned.1.call-done, bf16[896,2048]{1,0:T(8,128)(2,1)} %param.7), kind=kOutput, calls=%fused_computation.15 | convolution fusion | flops 6576668672 | bytes 17432576 | tf_op jit(solution)/shard_map/dot_general | solution.py:8
  123.8 0.0 copy-start
  123.8 0.0 copy-start.1
  123.8 0.0 reduce-scatter.2.cloned.1.call-update
  123.8 0.0 all-gather.3.cloned.1.call-start
  123.9 131.8 %reduce-scatter.2.cloned.1.call-done = f32[224,896]{1,0:T(8,128)} async-done(((f32[1792,896]{1,0:T(8,128)}), f32[224,896]{1,0:T(8,128)}) %reduce-scatter.2.cloned.1.call-update) | async-done | bytes 802832 | tf_op jit(solution)/shard_map/reduce_scatter | solution.py:32
  255.7 0.0 copy-done
  255.7 0.0 copy-done.1
  255.7 2.5 multiply_convert_fusion
  258.2 0.0 all-gather.3.cloned.1.call-update
  258.2 75.0 %all-gather.3.cloned.1.call-done = bf16[1792,896]{1,0:T(8,128)(2,1)} async-done(((bf16[224,896]{1,0:T(8,128)(2,1)}), bf16[1792,896]{1,0:T(8,128)(2,1)}) %all-gather.3.cloned.1.call-update) | async-done | bytes 3211280 | tf_op jit(solution)/shard_map/all_gather | solution.py:34
  333.3 11.3 %convolution_convert_fusion = bf16[896,2048]{1,0:T(8,128)(2,1)} fusion(bf16[1792,896]{1,0:T(8,128)(2,1)} %all-gather.3.cloned.1.call-done, bf16[1792,2048]{1,0:T(8,128)(2,1)} %all-gather.5.cloned.1.call-done), kind=kOutput, calls=%fused_computation | convolution fusion | flops 6578503680 | bytes 14221312 | tf_op jit(solution)/shard_map/dot_general | solution.py:14
Async XLA Ops:
  7.2 103.7 %all-gather.5.cloned.1.call-start = ((), (), s32[]{:S(2)}) async-start(), calls=%async_computation.2 | async-start | bytes 7569408 | tf_op jit(solution)/shard_map/all_gather | solution.py:31
  7.9 247.8 %reduce-scatter.2.cloned.1.call-start = ((), (), s32[]{:S(2)}) async-start(), calls=%async_computation.3 | async-start | bytes 7225344 | tf_op jit(solution)/shard_map/reduce_scatter | solution.py:32
  123.8 131.9 %copy-start = (bf16[224,896]{1,0:T(8,128)(2,1)S(1)}, bf16[224,896]{1,0:T(8,128)(2,1)}, u32[]{:S(2)}) copy-start(bf16[224,896]{1,0:T(8,128)(2,1)} %param.5) | copy-start | bytes 1204228
  123.8 131.9 %copy-start.1 = (bf16[224,896]{1,0:T(8,128)(2,1)S(1)}, bf16[224,896]{1,0:T(8,128)(2,1)}, u32[]{:S(2)}) copy-start(bf16[224,896]{1,0:T(8,128)(2,1)} %param.6) | copy-start | bytes 1204228
  123.8 209.4 %all-gather.3.cloned.1.call-start = ((), (), s32[]{:S(2)}) async-start(), calls=%async_computation.1 | async-start | bytes 3612672 | tf_op jit(solution)/shard_map/all_gather | solution.py:34
Sparse Core Ops, SparseCore 0:
  10.8 100.0 all-gather.4
  123.9 131.6 reduce-scatter.1
  258.4 74.8 all-gather.2
where the time goes:
time: 354 us; the launch traced here: 351 us
  waiting for transfers between devices  310 us (88%)
  matrix products  24.3 us (7%)
  between operations  13.7 us (4%)
    reduce_scatter x1, waiting for transfers between devices, on_device(): lax.psum_scatter(times_weight(panel, w_down), 'col', scatter_dimension=0,...  132 us
    all_gather x1, waiting for transfers between devices, on_device(): panel = lax.all_gather(out_grad, 'row', axis=0, tiled=True)  103 us
    all_gather x1, waiting for transfers between devices, on_device(): hidden_all = lax.all_gather(hidden, 'col', axis=0, tiled=True)  75 us
    dot_general x1, matrix products, times_weight(): lax.dot_general(panel, weight, (((1,), (1,)), ((), ())), preferred_elemen...  12.9 us
    dot_general x1, matrix products, token_contract(): lax.dot_general(left, right, (((0,), (0,)), ((), ())), preferred_element_...  11.3 us
  transfers between devices with their start and end apart: 3, of which 3 were waited for; matrix products, arithmetic and copies ran while one was open for 0% of the time, Pallas kernels for 0%

commit v1 on v0

v1 whole, which is shorter than its diff:
```python
import jax
import jax.numpy as jnp
from jax import lax
from jax.experimental import pallas as pl
from jax.experimental.pallas import tpu as pltpu
from jax.sharding import PartitionSpec as P

MESH = pl.DeviceIdType.MESH
BF = jnp.bfloat16
F32 = jnp.float32

TB = 56
UT = 112
H = 896
D = 2048
OT = 224
N1 = 8
N2 = 4
DT = D // N2


def wrap(a, n):
    return lax.rem(a + n, n)


def table(i, values):
    total = jnp.int32(0)
    for k, v in enumerate(values):
        if v != 0:
            total = total + jnp.where(i == k, v, 0)
    return total


MERGED = [0, 1, 1, 3, 3, 5, 5, 7, 8, 8, 8, 8]
SUMMED = [0, 0, 0, 1, 1, 3, 3, 5, 7, 8, 8, 8]
FINISHED = [0, 0, 0, 0, 0, 1, 1, 3, 5, 7, 7, 8]


def kernel(
    og, gate, up, w_hbm, gd_out, gg_out, gu_out,
    panel, w, wt, part, hid, far, near, cross, mine, gate_v, up_v, f_up, f_gate, gg_v, gu_v,
    in_sem, out_sem, gd_sem, ring_recv, sib_recv, up_send, dn_send, sib_send, xh_send,
    hid_recv, half_recv, hy_send, half_send, hx_send,
    far_recv, near_recv, first_send, merge_send, cross_recv, cross_send,
):
    row = lax.axis_index("row")
    col = lax.axis_index("col")
    xh = lax.div(row, 16)
    z = lax.rem(lax.div(row, 2), 8)
    core = lax.rem(row, 2)
    y = lax.div(col, 2)
    xl = lax.rem(col, 2)

    def at(xh_, z_, core_, y_, xl_):
        return ((xh_ * 8 + z_) * 2 + core_, y_ * 2 + xl_)

    z_up = at(xh, wrap(z + 1, 8), core, y, xl)
    z_dn = at(xh, wrap(z - 1, 8), core, y, xl)
    x_far = at(1 - xh, z, core, y, xl)
    sib = at(xh, z, 1 - core, y, xl)
    y_up = at(xh, z, core, wrap(y + 1, 4), xl)
    y_dn = at(xh, z, core, wrap(y - 1, 4), xl)
    x_near = at(xh, z, core, y, 1 - xl)

    def remote(src, dst, ssem, rsem, dev):
        return pltpu.make_async_remote_copy(
            src_ref=src, dst_ref=dst, send_sem=ssem, recv_sem=rsem, device_id=dev, device_id_type=MESH
        )

    load_gate = pltpu.make_async_copy(gate, gate_v, in_sem.at[0])
    load_up = pltpu.make_async_copy(up, up_v, in_sem.at[1])
    load_w = pltpu.make_async_copy(w_hbm, w, in_sem.at[2])
    own_unit = xh * 8 + z
    own_block = own_unit * 2 + core
    load_og = pltpu.make_async_copy(og, panel.at[own_block], in_sem.at[3])

    barrier = pltpu.get_barrier_semaphore()
    for dev in (z_up, z_dn, x_far, sib, y_up, y_dn, x_near):
        pl.semaphore_signal(barrier, inc=1, device_id=dev, device_id_type=MESH)
    load_gate.start()
    load_up.start()
    load_og.start()
    load_w.start()
    pl.semaphore_wait(barrier, 7)

    def ring_copy(unit, ssem, dev, src=None):
        block = panel.at[unit * 2 + core]
        return remote(block if src is None else src, block, ssem.at[unit], ring_recv.at[unit], dev)

    def go_up(unit, src=None):
        return ring_copy(unit, up_send, z_up, src)

    def go_dn(unit, src=None):
        return ring_copy(unit, dn_send, z_dn, src)

    def to_sib(unit, src=None):
        block = panel.at[unit * 2 + core]
        return remote(block if src is None else src, block, sib_send.at[unit], sib_recv.at[unit], sib)

    def from_sib(unit):
        block = panel.at[unit * 2 + 1 - core]
        return remote(block, block, sib_send.at[unit], sib_recv.at[unit], sib)

    def to_far():
        return remote(og, panel.at[own_block], xh_send, ring_recv.at[own_unit], x_far)

    go_up(own_unit, og).start()
    go_dn(own_unit, og).start()
    to_far().start()
    to_sib(own_unit, og).start()

    def hid_copy(c, ssem, dev):
        return remote(hid.at[c], hid.at[c], ssem, hid_recv.at[c], dev)

    def half_copy(c, k, dev):
        block = hid.at[c, pl.ds(UT * k, UT)]
        return remote(block, block, half_send.at[k], half_recv.at[k], dev)

    def hx_copy(y_):
        return hid_copy(y_ * 2 + xl, hx_send.at[y_], x_near)

    y_next, y_prev, y_opp = wrap(y + 1, 4), wrap(y - 1, 4), wrap(y + 2, 4)

    load_gate.wait()
    load_up.wait()

    @pl.loop(0, OT // 16)
    def _(k):
        rows = pl.ds(pl.multiple_of(k * 16, 16), 16)
        g = gate_v[rows, :].astype(F32)
        u = up_v[rows, :].astype(F32)
        s = 1.0 / (1.0 + jnp.exp(-g))
        silu = g * s
        hid[col, rows, :] = (silu * u).astype(BF)
        f_up[rows, :] = silu
        f_gate[rows, :] = u * s * (1.0 + g * (1.0 - s))

    hid_copy(col, hy_send.at[0], y_up).start()
    hid_copy(col, hy_send.at[1], y_dn).start()
    hx_copy(y).start()

    load_w.wait()

    @pl.loop(0, 8)
    def _(k):
        cols = pl.ds(pl.multiple_of(k * 256, 256), 256)
        wt[cols, :] = w[:, cols].T

    far_unit = (1 - xh) * 8 + z
    ring_copy(far_unit, up_send, z_up).wait_recv()
    go_up(far_unit).start()
    go_dn(far_unit).start()
    to_sib(far_unit).start()
    load_og.wait()

    def pass_on(d, xh_):
        from_dn = xh_ * 8 + wrap(z - d, 8)
        go_up(from_dn).wait_recv()

        @pl.when(jnp.logical_or(d < 3, xh_ == 0))
        def _():
            go_up(from_dn).start()

        to_sib(from_dn).start()
        from_up = xh_ * 8 + wrap(z + d, 8)
        go_dn(from_up).wait_recv()

        @pl.when(jnp.logical_or(d < 3, xh_ == 1))
        def _():
            go_dn(from_up).start()

        to_sib(from_up).start()

    def z_of(q):
        return wrap(z + lax.div(q + 1, 2) * (1 - 2 * lax.rem(q, 2)), 8)

    y_half = lax.div(y, 2)

    def at_end(zq):
        return lax.div(zq, 4) == lax.rem(y, 2)

    def far_copy(zq, dev):
        unit = (1 - y_half) * 8 + zq
        return remote(part.at[unit], far.at[lax.rem(zq, 4)], first_send.at[zq], far_recv.at[lax.rem(zq, 4)], dev)

    def near_copy(y_to, side, zq, sem, dev):
        unit = lax.div(y_to, 2) * 8 + zq
        k = lax.rem(zq, 4)
        return remote(part.at[unit], near.at[side, k], sem, near_recv.at[side, k], dev)

    def first_sends(zq):
        even = lax.rem(zq, 2) == 0
        end = at_end(zq)

        @pl.when(jnp.logical_and(end, even))
        def _():
            far_copy(zq, y_dn).start()

        @pl.when(jnp.logical_and(end, jnp.logical_not(even)))
        def _():
            far_copy(zq, y_up).start()

        @pl.when(jnp.logical_and(jnp.logical_not(end), even))
        def _():
            near_copy(y_next, 0, zq, first_send.at[zq], y_up).start()

        @pl.when(jnp.logical_and(jnp.logical_not(end), jnp.logical_not(even)))
        def _():
            near_copy(y_prev, 1, zq, first_send.at[zq], y_dn).start()

    def merge(zq):
        @pl.when(jnp.logical_not(at_end(zq)))
        def _():
            k = lax.rem(zq, 4)
            even = lax.rem(zq, 2) == 0
            y_to = jnp.where(even, y_prev, y_next)
            unit = lax.div(y_to, 2) * 8 + zq
            far_copy(zq, y_up).wait_recv()

            @pl.loop(0, UT // 16)
            def _(r):
                rows = pl.ds(pl.multiple_of(r * 16, 16), 16)
                part[unit, rows, :] = (part[unit, rows, :].astype(F32) + far[k, rows, :].astype(F32)).astype(BF)

            @pl.when(even)
            def _():
                near_copy(y_prev, 1, zq, merge_send.at[k], y_dn).start()

            @pl.when(jnp.logical_not(even))
            def _():
                near_copy(y_next, 0, zq, merge_send.at[k], y_up).start()

    def is_mine(zq):
        return lax.rem(lax.div(zq, 2), 2) == xl

    def cross_copy(zq):
        k = lax.rem(zq, 2)
        return remote(part.at[y_half * 8 + zq], cross.at[k], cross_send.at[k], cross_recv.at[k], x_near)

    def sum_up(zq):
        @pl.when(at_end(zq))
        def _():
            k = lax.rem(zq, 4)
            unit = y_half * 8 + zq
            near_copy(y, 0, zq, first_send.at[zq], y_dn).wait_recv()
            near_copy(y, 1, zq, first_send.at[zq], y_up).wait_recv()
            own = is_mine(zq)

            def total(rows):
                return part[unit, rows, :].astype(F32) + (
                    near[0, k, rows, :].astype(F32) + near[1, k, rows, :].astype(F32)
                )

            @pl.when(own)
            def _():
                @pl.loop(0, UT // 16)
                def _(r):
                    rows = pl.ds(pl.multiple_of(r * 16, 16), 16)
                    mine[lax.rem(zq, 2), rows, :] = total(rows)

            @pl.when(jnp.logical_not(own))
            def _():
                @pl.loop(0, UT // 16)
                def _(r):
                    rows = pl.ds(pl.multiple_of(r * 16, 16), 16)
                    part[unit, rows, :] = total(rows).astype(BF)

                cross_copy(zq).start()

    def out_copies(k):
        rows = pl.ds(pl.multiple_of(k * UT, 16), UT)
        return (
            pltpu.make_async_copy(gg_v.at[rows], gg_out.at[rows], out_sem.at[0, k]),
            pltpu.make_async_copy(gu_v.at[rows], gu_out.at[rows], out_sem.at[1, k]),
        )

    def finish(zq):
        @pl.when(jnp.logical_and(at_end(zq), is_mine(zq)))
        def _():
            k = lax.rem(zq, 2)
            cross_copy(zq).wait_recv()

            @pl.loop(0, UT // 16)
            def _(r):
                rows = pl.ds(pl.multiple_of(r * 16, 16), 16)
                here = pl.ds(pl.multiple_of(k * UT + r * 16, 16), 16)
                grad = mine[k, rows, :] + cross[k, rows, :].astype(F32)
                gu_v[here, :] = (grad * f_up[here, :]).astype(BF)
                gg_v[here, :] = (grad * f_gate[here, :]).astype(BF)

            for c in out_copies(k):
                c.start()

    def gd_copy(t):
        cols = pl.ds(pl.multiple_of(t * DT, DT), DT)
        return pltpu.make_async_copy(w.at[:, cols], gd_out.at[:, cols], gd_sem.at[t])

    @pl.loop(0, N1 + N2)
    def _(i):
        odd = lax.rem(i, 2) == 1

        @pl.when(jnp.logical_and(odd, i < 7))
        def _():
            d = lax.div(i + 1, 2)
            pass_on(d, xh)
            pass_on(d, 1 - xh)

        z_opp = wrap(z + 4, 8)

        @pl.when(i == 7)
        def _():
            go_up(z_opp).wait_recv()
            to_sib(z_opp).start()
            go_dn(8 + z_opp).wait_recv()
            to_sib(8 + z_opp).start()

        @pl.when(i < N1)
        def _():
            zq = z_of(i)
            from_sib(zq).wait_recv()
            from_sib(8 + zq).wait_recv()
            lhs = jnp.concatenate(
                [panel[pl.ds(2 * zq, 2)].reshape(UT, D), panel[pl.ds(16 + 2 * zq, 2)].reshape(UT, D)], axis=0
            )
            res = lax.dot_general(lhs, wt[...], (((1,), (0,)), ((), ())), preferred_element_type=F32).astype(BF)
            part[zq] = res[:UT]
            part[8 + zq] = res[UT:]
            first_sends(zq)

        @pl.when(i == 1)
        def _():
            hid_copy(y_next * 2 + xl, hy_send.at[0], y_up).wait_recv()
            half_copy(y_next * 2 + xl, 0, y_dn).start()
            hx_copy(y_next).start()
            hid_copy(y_prev * 2 + xl, hy_send.at[1], y_dn).wait_recv()
            half_copy(y_prev * 2 + xl, 1, y_up).start()
            hx_copy(y_prev).start()

        @pl.when(i == 3)
        def _():
            half_copy(y_opp * 2 + xl, 0, y_up).wait_recv()
            half_copy(y_opp * 2 + xl, 1, y_dn).wait_recv()
            hx_copy(y_opp).start()

        @pl.when(i == N1)
        def _():
            for y_ in range(4):
                hid_copy(y_ * 2 + 1 - xl, hx_send.at[y_], x_near).wait_recv()

        @pl.when(i >= N1)
        def _():
            t = i - N1
            cols = pl.ds(pl.multiple_of(t * DT, DT), DT)
            res = lax.dot_general(
                hid[...].reshape(8 * OT, H),
                panel[:, :, cols].reshape(8 * OT, DT),
                (((0,), (0,)), ((), ())),
                preferred_element_type=F32,
            )
            w[:, cols] = res.astype(BF)
            gd_copy(t).start()

        before = jnp.maximum(i - 1, 0)

        @pl.loop(table(before, MERGED), table(i, MERGED))
        def _(q):
            merge(z_of(q))

        @pl.loop(table(before, SUMMED), table(i, SUMMED))
        def _(q):
            sum_up(z_of(q))

        @pl.loop(table(before, FINISHED), table(i, FINISHED))
        def _(q):
            finish(z_of(q))

    to_far().wait_send()

    @pl.loop(0, 4)
    def _(d):
        for xh_ in range(2):
            below = xh_ * 8 + wrap(z - d, 8)
            above = xh_ * 8 + wrap(z + d, 8)

            @pl.when(jnp.logical_or(d < 3, xh_ == 0))
            def _():
                go_up(below).wait_send()

            @pl.when(jnp.logical_or(d < 3, xh_ == 1))
            def _():
                go_dn(above).wait_send()

    @pl.loop(0, 16)
    def _(u):
        to_sib(u).wait_send()

    hid_copy(col, hy_send.at[0], y_up).wait_send()
    hid_copy(col, hy_send.at[1], y_dn).wait_send()
    half_copy(col, 0, y_dn).wait_send()
    half_copy(col, 1, y_up).wait_send()
    for y_ in range(4):
        hx_copy(y_).wait_send()

    @pl.loop(0, 8)
    def _(zq):
        far_copy(zq, y_up).wait_send()

        @pl.when(jnp.logical_not(at_end(zq)))
        def _():
            near_copy(y_next, 0, zq, merge_send.at[lax.rem(zq, 4)], y_up).wait_send()

    for k in range(2):
        cross_copy(k).wait_send()
        for c in out_copies(k):
            c.wait()
    for t in range(N2):
        gd_copy(t).wait()


def on_device(out_grad, gate_pre, up_pre, w_down):
    dma = pltpu.SemaphoreType.DMA
    any_space = pl.BlockSpec(memory_space=pl.ANY)
    return pl.pallas_call(
        kernel,
        out_shape=(
            jax.ShapeDtypeStruct((H, D), BF),
            jax.ShapeDtypeStruct((OT, H), BF),
            jax.ShapeDtypeStruct((OT, H), BF),
        ),
        in_specs=[any_space] * 4,
        out_specs=(any_space,) * 3,
        scratch_shapes=[
            pltpu.VMEM((32, TB, D), BF),
            pltpu.VMEM((H, D), BF),
            pltpu.VMEM((D, H), BF),
            pltpu.VMEM((16, UT, H), BF),
            pltpu.VMEM((8, OT, H), BF),
            pltpu.VMEM((4, UT, H), BF),
            pltpu.VMEM((2, 4, UT, H), BF),
            pltpu.VMEM((2, UT, H), BF),
            pltpu.VMEM((2, UT, H), F32),
            pltpu.VMEM((OT, H), BF),
            pltpu.VMEM((OT, H), BF),
            pltpu.VMEM((OT, H), F32),
            pltpu.VMEM((OT, H), F32),
            pltpu.VMEM((OT, H), BF),
            pltpu.VMEM((OT, H), BF),
            dma((4,)), dma((2, 2)), dma((N2,)),
            dma((16,)), dma((16,)), dma((16,)), dma((16,)), dma((16,)), dma,
            dma((8,)), dma((2,)), dma((2,)), dma((2,)), dma((4,)),
            dma((4,)), dma((2, 4)), dma((8,)), dma((4,)), dma((2,)), dma((2,)),
        ],
        compiler_params=pltpu.CompilerParams(
            collective_id=0, has_side_effects=True, vmem_limit_bytes=56 * 2**20
        ),
        cost_estimate=pl.CostEstimate(flops=4 * 1792 * H * D, bytes_accessed=9 * 2**20, transcendentals=OT * H),
        name="swiglu_down_backward",
    )(out_grad, gate_pre, up_pre, w_down)


def solution(mesh):
    return jax.shard_map(
        on_device,
        mesh=mesh,
        in_specs=(P("row", "col"), P("col", "row"), P("col", "row"), P("row", "col")),
        out_specs=(P("row", "col"), P("col", "row"), P("col", "row")),
        check_vma=False,
    )
```

time: 354 us -> 89.7 us (0.25)
  waiting for transfers between devices: 310 us -> 0 us
  Pallas kernels: 0 us -> 81.4 us
  matrix products: 24.3 us -> 0 us
  between operations: 13.7 us -> 0.66 us
  local copies, waits for them, and re-layouts: 0.01 us -> 5.95 us
    all_gather x2 -> x0, waiting for transfers between devices: 178 us -> none  [the longest x1 103 us: on_device(): panel = lax.all_gather(out_grad, 'row', axis=0, tiled=True)]
    reduce_scatter x1 -> x0, waiting for transfers between devices: 132 us -> none  [on_device(): lax.psum_scatter(times_weight(panel, w_down), 'col', scatter_dimension=0,...]
    pallas_call x0 -> x1, Pallas kernels: none -> 81.4 us  [on_device(): pl.pallas_call(kernel, out_shape=(jax.ShapeDtypeStruct((H, D), BF), jax.S...]
    dot_general x2 -> x0, matrix products: 24.3 us -> none  [the longest x1 12.9 us: times_weight(): lax.dot_general(panel, weight, (((1,), (1,)), ((), ())), preferred_elemen...]
    unnamed x4 -> x7, local copies, waits for them, and re-layouts: 0.01 us -> 5.95 us
  transfers between devices with their start and end apart: 3 -> 0, of which waited for: 3 -> 0; matrix products, arithmetic and copies ran while one was open for 0% -> 0% of each run, Pallas kernels for 0% -> 0%
where the time goes in v1:
time: 89.7 us; the launch traced here: 88 us
  Pallas kernels  81.4 us (91%)
  local copies, waits for them, and re-layouts  5.95 us (7%)
    pallas_call x1, Pallas kernels, on_device(): pl.pallas_call(kernel, out_shape=(jax.ShapeDtypeStruct((H, D), BF), jax.S...  81.4 us
    unnamed x7, local copies, waits for them, and re-layouts  5.95 us

profile of v1, /device:TPU:40, one launch (start us, length us, event | category | flops | bytes accessed | tf_op | source)
XLA Modules:
  0.0 88.0 jit_solution(13446706067361072763)
XLA Ops:
  0.6 81.4 %swiglu_down_backward.1 = (bf16[896,2048]{1,0:T(8,128)(2,1)}, bf16[224,896]{1,0:T(8,128)(2,1)}, bf16[224,896]{1,0:T(8,128)(2,1)}) custom-call(bf16[56,2048]{1,0:T(8,128)(2,1)} %og.1, bf16[224,896]{1,0:T(8,128)(2,1)} %gate.1, bf16[224,896]{1,0:T(8,128)(2,1)} %up.1, bf16[896,2048]{1,0:T(8,128)(2,1)} %w_hbm.1), custom_call_target="tpu_custom_call" | custom-call | flops 13153337344 | bytes 9437184 | tf_op jit(solution)/shard_map/swiglu_down_backward/pallas_call | solution.py:423
  82.1 0.0 copy-start.1
  82.1 0.0 copy-start
  82.1 4.4 %copy.10 = bf16[896,2048]{1,0:T(8,128)(2,1)} copy(bf16[896,2048]{1,0:T(8,128)(2,1)} %get-tuple-element.6) | data formatting | bytes 7340032
  86.5 0.0 copy-done.1
  86.5 0.7 copy.11
  87.3 0.0 copy-done
  87.3 0.7 copy.12
Async XLA Ops:
  82.1 4.5 %copy-start.1 = (bf16[224,896]{1,0:T(8,128)(2,1)S(1)}, bf16[224,896]{1,0:T(8,128)(2,1)}, u32[]{:S(2)}) copy-start(bf16[224,896]{1,0:T(8,128)(2,1)} %get-tuple-element.7) | copy-start | bytes 1204228
  82.1 5.2 %copy-start = (bf16[224,896]{1,0:T(8,128)(2,1)S(1)}, bf16[224,896]{1,0:T(8,128)(2,1)}, u32[]{:S(2)}) copy-start(bf16[224,896]{1,0:T(8,128)(2,1)} %get-tuple-element.8) | copy-start | bytes 1204228

commit v2 on v0

v2 whole, which is shorter than its diff:
```python
import jax
import jax.numpy as jnp
from jax import lax
from jax.experimental import pallas as pl
from jax.experimental.pallas import tpu as pltpu
from jax.sharding import PartitionSpec as P

MESH = pl.DeviceIdType.MESH
BF = jnp.bfloat16
F32 = jnp.float32

TB = 56
UT = 112
HALVES = ((0, 64), (64, 48))
H = 896
D = 2048
DH = D // 2
OT = 224
N1 = 9
N2 = 4
DT = D // N2


def wrap(a, n):
    return lax.rem(a + n, n)


def table(i, values):
    total = jnp.int32(0)
    for k, v in enumerate(values):
        if v != 0:
            total = total + jnp.where(i == k, v, 0)
    return total


MERGED = [0, 0, 2, 3, 5, 7, 9, 9, 14, 16, 16, 16, 16]
SUMMED = [0, 0, 0, 0, 2, 3, 5, 5, 9, 14, 16, 16, 16]
FINISHED = [0, 0, 0, 0, 0, 0, 2, 2, 5, 9, 14, 14, 16]
HID_NEAR = 2
HID_FAR = 4


def kernel(
    og, gate, up, w_hbm, gd_out, gg_out, gu_out,
    panel, w, wt, part, hid, far, near, cross, mine, gate_v, up_v, f_up, f_gate,
    in_sem, ring_recv, sib_recv, up_send, dn_send, sib_send, xh_send,
    hid_recv, hup_send, hdn_send, hx_send,
    far_recv, near_recv, first_send, merge_send, cross_recv, cross_send,
):
    row = lax.axis_index("row")
    col = lax.axis_index("col")
    xh = lax.div(row, 16)
    z = lax.rem(lax.div(row, 2), 8)
    core = lax.rem(row, 2)
    y = lax.div(col, 2)
    xl = lax.rem(col, 2)

    def at(xh_, z_, core_, y_, xl_):
        return ((xh_ * 8 + z_) * 2 + core_, y_ * 2 + xl_)

    y_next, y_prev, y_opp = wrap(y + 1, 4), wrap(y - 1, 4), wrap(y + 2, 4)
    z_up = at(xh, wrap(z + 1, 8), core, y, xl)
    z_dn = at(xh, wrap(z - 1, 8), core, y, xl)
    x_far = at(1 - xh, z, core, y, xl)
    sib = at(xh, z, 1 - core, y, xl)
    y_up = at(xh, z, core, y_next, xl)
    y_dn = at(xh, z, core, y_prev, xl)
    x_near = at(xh, z, core, y, 1 - xl)

    def remote(src, dst, ssem, rsem, dev):
        return pltpu.make_async_remote_copy(
            src_ref=src, dst_ref=dst, send_sem=ssem, recv_sem=rsem, device_id=dev, device_id_type=MESH
        )

    load_gate = pltpu.make_async_copy(gate, gate_v, in_sem.at[0])
    load_up = pltpu.make_async_copy(up, up_v, in_sem.at[1])
    load_w = pltpu.make_async_copy(w_hbm, w, in_sem.at[2])
    own_unit = xh * 8 + z
    far_unit = (1 - xh) * 8 + z
    load_og = pltpu.make_async_copy(og, panel.at[own_unit * 2 + core], in_sem.at[3])

    barrier = pltpu.get_barrier_semaphore()
    for dev in (z_up, z_dn, x_far, sib, y_up, y_dn, x_near):
        pl.semaphore_signal(barrier, inc=1, device_id=dev, device_id_type=MESH)
    load_gate.start()
    load_up.start()
    load_og.start()
    load_w.start()
    pl.semaphore_wait(barrier, 7)

    def half(j):
        return pl.ds(j * DH, DH)

    def ring_copy(unit, j, ssem, dev, own=False):
        block = panel.at[unit * 2 + core, :, half(j)]
        return remote(og.at[:, half(j)] if own else block, block, ssem, ring_recv.at[j, unit], dev)

    def go_up(unit, j, own=False):
        return ring_copy(unit, j, up_send.at[j, unit], z_up, own)

    def go_dn(unit, j, own=False):
        return ring_copy(unit, j, dn_send.at[j, unit], z_dn, own)

    def to_far(j):
        return ring_copy(own_unit, j, xh_send.at[j], x_far, True)

    def sib_copy(unit, j, core_, own=False):
        block = panel.at[unit * 2 + core_, :, half(j)]
        return remote(
            og.at[:, half(j)] if own else block, block, sib_send.at[j, unit], sib_recv.at[j, unit], sib
        )

    def to_sib(unit, j, own=False):
        return sib_copy(unit, j, core, own)

    for j in range(2):
        to_far(j).start()
        go_up(own_unit, j, True).start()
        go_dn(own_unit, j, True).start()
    for j in range(2):
        to_sib(own_unit, j, True).start()

    def hid_copy(c, ssem, dev):
        return remote(hid.at[c], hid.at[c], ssem, hid_recv.at[c], dev)

    load_gate.wait()
    load_up.wait()

    @pl.loop(0, OT // 16)
    def _(k):
        rows = pl.ds(pl.multiple_of(k * 16, 16), 16)
        g = gate_v[rows, :].astype(F32)
        u = up_v[rows, :].astype(F32)
        s = 1.0 / (1.0 + jnp.exp(-g))
        silu = g * s
        hid[col, rows, :] = (silu * u).astype(BF)
        f_up[rows, :] = silu
        f_gate[rows, :] = u * s * (1.0 + g * (1.0 - s))

    c_next, c_prev, c_opp = y_next * 2 + xl, y_prev * 2 + xl, y_opp * 2 + xl
    p_own, p_next, p_prev, p_opp = (y_ * 2 + 1 - xl for y_ in (y, y_next, y_prev, y_opp))
    hid_copy(col, hup_send.at[0], y_up).start()
    hid_copy(col, hdn_send.at[0], y_dn).start()
    hid_copy(col, hx_send.at[0], x_near).start()

    def pass_on(d, xh_):
        from_dn = xh_ * 8 + wrap(z - d, 8)
        from_up = xh_ * 8 + wrap(z + d, 8)
        for j in range(2):
            go_up(from_dn, j).wait_recv()

            @pl.when(jnp.logical_or(d < 3, xh_ == 0))
            def _():
                go_up(from_dn, j).start()

            to_sib(from_dn, j).start()
            go_dn(from_up, j).wait_recv()

            @pl.when(jnp.logical_or(d < 3, xh_ == 1))
            def _():
                go_dn(from_up, j).start()

            to_sib(from_up, j).start()

    for j in range(2):
        to_far_in = ring_copy(far_unit, j, xh_send.at[j], x_far)
        to_far_in.wait_recv()
        go_up(far_unit, j).start()
        go_dn(far_unit, j).start()
        to_sib(far_unit, j).start()
    pass_on(1, xh)

    load_w.wait()

    @pl.loop(0, 8)
    def _(k):
        cols = pl.ds(pl.multiple_of(k * 256, 256), 256)
        wt[cols, :] = w[:, cols].T

    load_og.wait()

    def unit(k):
        d = lax.div(k + 2, 4)
        own = jnp.logical_or(k == 0, jnp.logical_and(lax.rem(k + 2, 4) < 2, k < 15))
        return jnp.where(own, xh, 1 - xh) * 8 + jnp.where(lax.rem(k, 2) == 0, wrap(z - d, 8), wrap(z + d, 8))

    def distance(m):
        return wrap(y - lax.div(m, 4), 4)

    def rows_of(hf):
        return pl.ds(HALVES[hf][0], HALVES[hf][1])

    def far_copy(m, hf, dev):
        k = hf * 4 + lax.rem(m, 4)
        return remote(
            part.at[m, rows_of(hf)], far.at[k, pl.ds(0, HALVES[hf][1])], first_send.at[hf, m], far_recv.at[k], dev
        )

    def near_copy(m, hf, side, sem, dev):
        k = lax.rem(m, 4)
        return remote(
            part.at[m, rows_of(hf)], near.at[side, k, rows_of(hf)], sem, near_recv.at[side, k, hf], dev
        )

    def first_sends(m):
        d = distance(m)

        @pl.when(d == 2)
        def _():
            far_copy(m, 0, y_dn).start()
            far_copy(m, 1, y_up).start()

        @pl.when(d == 1)
        def _():
            near_copy(m, 1, 1, first_send.at[1, m], y_dn).start()

        @pl.when(d == 3)
        def _():
            near_copy(m, 0, 0, first_send.at[0, m], y_up).start()

    def row_loop(hf):
        return pl.loop(0, HALVES[hf][1] // 16)

    def merge(m):
        d = distance(m)
        for hf in range(2):

            @pl.when(d == 1 + 2 * hf)
            def _():
                far_copy(m, hf, y_up if hf == 0 else y_dn).wait_recv()
                k = hf * 4 + lax.rem(m, 4)

                @row_loop(hf)
                def _(r):
                    rows = pl.ds(pl.multiple_of(HALVES[hf][0] + r * 16, 16), 16)
                    theirs = far[k, pl.ds(pl.multiple_of(r * 16, 16), 16), :]
                    part[m, rows, :] = (part[m, rows, :].astype(F32) + theirs.astype(F32)).astype(BF)

                near_copy(m, hf, 1 - hf, merge_send.at[m], y_dn if hf == 0 else y_up).start()

    def is_mine(m):
        return lax.rem(lax.div(m, 2), 2) == xl

    def cross_copy(m, hf):
        k = lax.rem(m, 2)
        return remote(
            part.at[m, rows_of(hf)], cross.at[k, rows_of(hf)], cross_send.at[k, hf], cross_recv.at[k, hf], x_near
        )

    def sum_up(m):
        @pl.when(distance(m) == 0)
        def _():
            k = lax.rem(m, 4)
            own = is_mine(m)
            for hf in range(2):
                near_copy(m, hf, 0, first_send.at[hf, m], y_dn).wait_recv()
                near_copy(m, hf, 1, first_send.at[hf, m], y_up).wait_recv()

                def total(r):
                    rows = pl.ds(pl.multiple_of(HALVES[hf][0] + r * 16, 16), 16)
                    sides = near[0, k, rows, :].astype(F32) + near[1, k, rows, :].astype(F32)
                    return rows, part[m, rows, :].astype(F32) + sides

                @pl.when(own)
                def _():
                    @row_loop(hf)
                    def _(r):
                        rows, value = total(r)
                        mine[lax.rem(m, 2), rows, :] = value

                @pl.when(jnp.logical_not(own))
                def _():
                    @row_loop(hf)
                    def _(r):
                        rows, value = total(r)
                        part[m, rows, :] = value.astype(BF)

                    cross_copy(m, hf).start()

    def finish(m):
        @pl.when(jnp.logical_and(distance(m) == 0, is_mine(m)))
        def _():
            k = lax.rem(m, 2)
            for hf in range(2):
                cross_copy(m, hf).wait_recv()

                @row_loop(hf)
                def _(r):
                    rows = pl.ds(pl.multiple_of(HALVES[hf][0] + r * 16, 16), 16)
                    here = pl.ds(pl.multiple_of(k * UT + HALVES[hf][0] + r * 16, 16), 16)
                    grad = mine[k, rows, :] + cross[k, rows, :].astype(F32)
                    gu_out[here, :] = (grad * f_up[here, :]).astype(BF)
                    gg_out[here, :] = (grad * f_gate[here, :]).astype(BF)

    @pl.loop(0, N1 + N2)
    def _(i):
        @pl.when(i < N1)
        def _():
            k0 = 2 * i - 1 + jnp.where(i < 2, 1, 0) - jnp.where(i == 8, 1, 0)
            both = jnp.logical_and(i != 1, i != 7)
            m0 = unit(k0)
            m1 = jnp.where(both, unit(k0 + 1), m0)
            for j in range(2):
                sib_copy(m0, j, 1 - core).wait_recv()

            @pl.when(both)
            def _():
                for j in range(2):
                    sib_copy(m1, j, 1 - core).wait_recv()

            lhs = jnp.concatenate(
                [panel[pl.ds(2 * m0, 2)].reshape(UT, D), panel[pl.ds(2 * m1, 2)].reshape(UT, D)], axis=0
            )
            res = lax.dot_general(lhs, wt[...], (((1,), (0,)), ((), ())), preferred_element_type=F32).astype(BF)
            part[m0] = res[:UT]
            first_sends(m0)

            @pl.when(both)
            def _():
                part[m1] = res[UT:]
                first_sends(m1)

        @pl.when(i == N1)
        def _():
            hid_copy(c_opp, hup_send.at[1], y_dn).wait_recv()
            hid_copy(p_own, hx_send.at[0], x_near).wait_recv()
            hid_copy(p_prev, hx_send.at[2], x_near).wait_recv()
            hid_copy(p_opp, hdn_send.at[1], y_up).wait_recv()

        @pl.when(i >= N1)
        def _():
            t = i - N1
            cols = pl.ds(pl.multiple_of(t * DT, DT), DT)
            res = lax.dot_general(
                hid[...].reshape(8 * OT, H),
                panel[:, :, cols].reshape(8 * OT, DT),
                (((0,), (0,)), ((), ())),
                preferred_element_type=F32,
            )
            gd_out[:, cols] = res.astype(BF)

        before = jnp.maximum(i - 1, 0)

        @pl.loop(table(before, MERGED), table(i, MERGED))
        def _(k):
            merge(unit(k))

        @pl.loop(table(before, SUMMED), table(i, SUMMED))
        def _(k):
            sum_up(unit(k))

        @pl.loop(table(before, FINISHED), table(i, FINISHED))
        def _(k):
            finish(unit(k))

        @pl.when(i == HID_NEAR)
        def _():
            hid_copy(c_next, hup_send.at[0], y_up).wait_recv()
            hid_copy(c_next, hx_send.at[1], x_near).start()
            hid_copy(c_prev, hdn_send.at[0], y_dn).wait_recv()
            hid_copy(c_prev, hup_send.at[1], y_up).start()
            hid_copy(c_prev, hx_send.at[2], x_near).start()

        @pl.when(i == HID_FAR)
        def _():
            hid_copy(p_next, hx_send.at[1], x_near).wait_recv()
            hid_copy(p_next, hdn_send.at[1], y_dn).start()

        @pl.when(jnp.logical_and(i >= 1, i < 6))
        def _():
            pass_on(lax.div(i + 2, 2), jnp.where(lax.rem(i, 2) == 0, xh, 1 - xh))

        @pl.when(i == 7)
        def _():
            z_opp = wrap(z + 4, 8)
            for j in range(2):
                go_up(z_opp, j).wait_recv()
                to_sib(z_opp, j).start()
                go_dn(8 + z_opp, j).wait_recv()
                to_sib(8 + z_opp, j).start()

    for j in range(2):
        to_far(j).wait_send()

    @pl.loop(0, 4)
    def _(d):
        for xh_ in range(2):
            below = xh_ * 8 + wrap(z - d, 8)
            above = xh_ * 8 + wrap(z + d, 8)

            @pl.when(jnp.logical_or(d < 3, xh_ == 0))
            def _():
                for j in range(2):
                    go_up(below, j).wait_send()

            @pl.when(jnp.logical_or(d < 3, xh_ == 1))
            def _():
                for j in range(2):
                    go_dn(above, j).wait_send()

    @pl.loop(0, 16)
    def _(m):
        for j in range(2):
            to_sib(m, j).wait_send()
        d = distance(m)

        @pl.when(d >= 2)
        def _():
            far_copy(m, 0, y_dn).wait_send()

        @pl.when(jnp.logical_or(d == 1, d == 2))
        def _():
            far_copy(m, 1, y_up).wait_send()

        for hf in range(2):

            @pl.when(d == 1 + 2 * hf)
            def _():
                near_copy(m, hf, 1 - hf, merge_send.at[m], y_dn if hf == 0 else y_up).wait_send()

    for k in range(2):
        hid_copy(col, hup_send.at[k], y_up).wait_send()
        hid_copy(col, hdn_send.at[k], y_dn).wait_send()
    for k in range(3):
        hid_copy(col, hx_send.at[k], x_near).wait_send()
    for k in range(2):
        for hf in range(2):
            cross_copy(k, hf).wait_send()


def on_device(out_grad, gate_pre, up_pre, w_down):
    dma = pltpu.SemaphoreType.DMA
    any_space = pl.BlockSpec(memory_space=pl.ANY)
    return pl.pallas_call(
        kernel,
        out_shape=(
            pltpu.VMEM((H, D), BF),
            pltpu.VMEM((OT, H), BF),
            pltpu.VMEM((OT, H), BF),
        ),
        in_specs=[any_space] * 4,
        out_specs=(pl.BlockSpec(memory_space=pltpu.VMEM),) * 3,
        scratch_shapes=[
            pltpu.VMEM((32, TB, D), BF),
            pltpu.VMEM((H, D), BF),
            pltpu.VMEM((D, H), BF),
            pltpu.VMEM((16, UT, H), BF),
            pltpu.VMEM((8, OT, H), BF),
            pltpu.VMEM((8, HALVES[0][1], H), BF),
            pltpu.VMEM((2, 4, UT, H), BF),
            pltpu.VMEM((2, UT, H), BF),
            pltpu.VMEM((2, UT, H), F32),
            pltpu.VMEM((OT, H), BF),
            pltpu.VMEM((OT, H), BF),
            pltpu.VMEM((OT, H), F32),
            pltpu.VMEM((OT, H), F32),
            dma((4,)),
            dma((2, 16)), dma((2, 16)), dma((2, 16)), dma((2, 16)), dma((2, 16)), dma((2,)),
            dma((8,)), dma((2,)), dma((2,)), dma((3,)),
            dma((8,)), dma((2, 4, 2)), dma((2, 16)), dma((16,)), dma((2, 2)), dma((2, 2)),
        ],
        compiler_params=pltpu.CompilerParams(
            collective_id=0, has_side_effects=True, vmem_limit_bytes=56 * 2**20
        ),
        cost_estimate=pl.CostEstimate(flops=4 * 1792 * H * D, bytes_accessed=9 * 2**20, transcendentals=OT * H),
        name="swiglu_down_backward",
    )(out_grad, gate_pre, up_pre, w_down)


def solution(mesh):
    return jax.shard_map(
        on_device,
        mesh=mesh,
        in_specs=(P("row", "col"), P("col", "row"), P("col", "row"), P("row", "col")),
        out_specs=(P("row", "col"), P("col", "row"), P("col", "row")),
        check_vma=False,
    )
```

time: 354 us -> 79.5 us (0.22)
  the two profiles are of different devices: /device:TPU:40 before, /device:TPU:7 now
where the time goes in v2:
time: 79.5 us; the launch traced here: 79.4 us
  Pallas kernels  75.4 us (95%)
  local copies, waits for them, and re-layouts  3.33 us (4%)
    pallas_call x1, Pallas kernels, on_device(): pl.pallas_call(kernel, out_shape=(pltpu.VMEM((H, D), BF), pltpu.VMEM((OT,...  75.4 us
    unnamed x3, local copies, waits for them, and re-layouts  3.33 us

profile of v2, /device:TPU:7, one launch (start us, length us, event | category | flops | bytes accessed | tf_op | source)
XLA Modules:
  0.0 79.4 jit_solution(3540735517670901531)
XLA Ops:
  0.6 75.4 %swiglu_down_backward.1 = (bf16[896,2048]{1,0:T(8,128)(2,1)S(1)}, bf16[224,896]{1,0:T(8,128)(2,1)S(1)}, bf16[224,896]{1,0:T(8,128)(2,1)S(1)}) custom-call(bf16[56,2048]{1,0:T(8,128)(2,1)} %og.1, bf16[224,896]{1,0:T(8,128)(2,1)} %gate.1, bf16[224,896]{1,0:T(8,128)(2,1)} %up.1, bf16[896,2048]{1,0:T(8,128)(2,1)} %w_hbm.1), custom_call_target="tpu_custom_call" | custom-call | flops 13153337344 | bytes 9437184 | tf_op jit(solution)/shard_map/swiglu_down_backward/pallas_call | solution.py:434
  76.1 1.8 %copy.10 = bf16[896,2048]{1,0:T(8,128)(2,1)} copy(bf16[896,2048]{1,0:T(8,128)(2,1)S(1)} %get-tuple-element.3) | data formatting | bytes 7340032
  77.9 0.7 copy.11
  78.7 0.7 copy.12

commit v3 on v2

--- a/solution.py
+++ b/solution.py
@@ -33,9 +33,9 @@
     return total
 
 
-MERGED = [0, 0, 2, 3, 5, 7, 9, 9, 14, 16, 16, 16, 16]
-SUMMED = [0, 0, 0, 0, 2, 3, 5, 5, 9, 14, 16, 16, 16]
-FINISHED = [0, 0, 0, 0, 0, 0, 2, 2, 5, 9, 14, 14, 16]
+MERGED = [0, 0, 2, 3, 5, 7, 9, 11, 11, 14, 16, 16, 16, 16]
+SUMMED = [0, 0, 0, 0, 2, 3, 5, 7, 7, 11, 14, 16, 16, 16]
+FINISHED = [0, 0, 0, 0, 0, 0, 2, 3, 3, 7, 11, 14, 14, 16]
 HID_NEAR = 2
 HID_FAR = 4
 
@@ -141,7 +141,6 @@
     p_own, p_next, p_prev, p_opp = (y_ * 2 + 1 - xl for y_ in (y, y_next, y_prev, y_opp))
     hid_copy(col, hup_send.at[0], y_up).start()
     hid_copy(col, hdn_send.at[0], y_dn).start()
-    hid_copy(col, hx_send.at[0], x_near).start()
 
     def pass_on(d, xh_):
         from_dn = xh_ * 8 + wrap(z - d, 8)
@@ -161,6 +160,13 @@
                 go_dn(from_up, j).start()
 
             to_sib(from_up, j).start()
+
+    load_w.wait()
+
+    @pl.loop(0, 8)
+    def _(k):
+        cols = pl.ds(pl.multiple_of(k * 256, 256), 256)
+        wt[cols, :] = w[:, cols].T
 
     for j in range(2):
         to_far_in = ring_copy(far_unit, j, xh_send.at[j], x_far)
@@ -168,14 +174,8 @@
         go_up(far_unit, j).start()
         go_dn(far_unit, j).start()
         to_sib(far_unit, j).start()
+    hid_copy(col, hx_send.at[0], x_near).start()
     pass_on(1, xh)
-
-    load_w.wait()
-
-    @pl.loop(0, 8)
-    def _(k):
-        cols = pl.ds(pl.multiple_of(k * 256, 256), 256)
-        wt[cols, :] = w[:, cols].T
 
     load_og.wait()
 
@@ -292,8 +292,22 @@
                     gu_out[here, :] = (grad * f_up[here, :]).astype(BF)
                     gg_out[here, :] = (grad * f_gate[here, :]).astype(BF)
 
-    @pl.loop(0, N1 + N2)
+    @pl.loop(0, N1 + N2 + 1)
     def _(i):
+        before = jnp.maximum(i - 1, 0)
+
+        @pl.loop(table(before, MERGED), table(i, MERGED))
+        def _(k):
+            merge(unit(k))
+
+        @pl.loop(table(before, SUMMED), table(i, SUMMED))
+        def _(k):
+            sum_up(unit(k))
+
+        @pl.loop(table(before, FINISHED), table(i, FINISHED))
+        def _(k):
+            finish(unit(k))
+
         @pl.when(i < N1)
         def _():
             k0 = 2 * i - 1 + jnp.where(i < 2, 1, 0) - jnp.where(i == 8, 1, 0)
@@ -327,7 +341,7 @@
             hid_copy(p_prev, hx_send.at[2], x_near).wait_recv()
             hid_copy(p_opp, hdn_send.at[1], y_up).wait_recv()
 
-        @pl.when(i >= N1)
+        @pl.when(jnp.logical_and(i >= N1, i < N1 + N2))
         def _():
             t = i - N1
             cols = pl.ds(pl.multiple_of(t * DT, DT), DT)
@@ -339,20 +353,6 @@
             )
             gd_out[:, cols] = res.astype(BF)
 
-        before = jnp.maximum(i - 1, 0)
-
-        @pl.loop(table(before, MERGED), table(i, MERGED))
-        def _(k):
-            merge(unit(k))
-
-        @pl.loop(table(before, SUMMED), table(i, SUMMED))
-        def _(k):
-            sum_up(unit(k))
-
-        @pl.loop(table(before, FINISHED), table(i, FINISHED))
-        def _(k):
-            finish(unit(k))
-
         @pl.when(i == HID_NEAR)
         def _():
             hid_copy(c_next, hup_send.at[0], y_up).wait_recv()
@@ -428,10 +428,29 @@
             cross_copy(k, hf).wait_send()
 
 
+W_PARTS = 4
+
+
+def write_out(gd, gg, gu, gd_out, gg_out, gu_out, gd_sem, sem):
+    n = H // W_PARTS
+    copies = [
+        pltpu.make_async_copy(gd.at[pl.ds(k * n, n)], gd_out.at[pl.ds(k * n, n)], gd_sem.at[k])
+        for k in range(W_PARTS)
+    ]
+    copies += [
+        pltpu.make_async_copy(gg, gg_out, sem.at[0]),
+        pltpu.make_async_copy(gu, gu_out, sem.at[1]),
+    ]
+    for c in copies:
+        c.start()
+    for c in copies:
+        c.wait()
+
+
 def on_device(out_grad, gate_pre, up_pre, w_down):
     dma = pltpu.SemaphoreType.DMA
     any_space = pl.BlockSpec(memory_space=pl.ANY)
-    return pl.pallas_call(
+    results = pl.pallas_call(
         kernel,
         out_shape=(
             pltpu.VMEM((H, D), BF),
@@ -465,6 +484,16 @@
         cost_estimate=pl.CostEstimate(flops=4 * 1792 * H * D, bytes_accessed=9 * 2**20, transcendentals=OT * H),
         name="swiglu_down_backward",
     )(out_grad, gate_pre, up_pre, w_down)
+    results = [pltpu.with_memory_space_constraint(r, pltpu.VMEM) for r in results]
+    return pl.pallas_call(
+        write_out,
+        out_shape=tuple(jax.ShapeDtypeStruct(r.shape, r.dtype) for r in results),
+        in_specs=[any_space] * 3,
+        out_specs=(any_space,) * 3,
+        scratch_shapes=[dma((W_PARTS,)), dma((2,))],
+        compiler_params=pltpu.CompilerParams(vmem_limit_bytes=2**20),
+        name="write_out",
+    )(*results)
 
 
 def solution(mesh):

time: 79.5 us -> 77.9 us (0.980)
  the two profiles are of different devices: /device:TPU:7 before, /device:TPU:40 now
where the time goes in v3:
time: 77.9 us; the launch traced here: 77.8 us
  Pallas kernels  77.2 us (99%)
    pallas_call x1, Pallas kernels, on_device(): pl.pallas_call(kernel, out_shape=(pltpu.VMEM((H, D), BF), pltpu.VMEM((OT,...  75.1 us
    pallas_call x1, Pallas kernels, on_device(): pl.pallas_call(write_out, out_shape=tuple((jax.ShapeDtypeStruct(r.shape,...  2.14 us

profile of v3, /device:TPU:40, one launch (start us, length us, event | category | flops | bytes accessed | tf_op | source)
XLA Modules:
  0.0 77.8 jit_solution(11186118964700890256)
XLA Ops:
  0.6 75.1 %swiglu_down_backward.1 = (bf16[896,2048]{1,0:T(8,128)(2,1)S(1)}, bf16[224,896]{1,0:T(8,128)(2,1)S(1)}, bf16[224,896]{1,0:T(8,128)(2,1)S(1)}) custom-call(bf16[56,2048]{1,0:T(8,128)(2,1)} %og.1, bf16[224,896]{1,0:T(8,128)(2,1)} %gate.1, bf16[224,896]{1,0:T(8,128)(2,1)} %up.1, bf16[896,2048]{1,0:T(8,128)(2,1)} %w_hbm.1), custom_call_target="tpu_custom_call" | custom-call | flops 13153337344 | bytes 9437184 | tf_op jit(solution)/shard_map/swiglu_down_backward/pallas_call | solution.py:453
  75.7 2.1 %write_out.1 = (bf16[896,2048]{1,0:T(8,128)(2,1)}, bf16[224,896]{1,0:T(8,128)(2,1)}, bf16[224,896]{1,0:T(8,128)(2,1)}) custom-call(bf16[896,2048]{1,0:T(8,128)(2,1)S(1)} %get-tuple-element.6.gd, bf16[224,896]{1,0:T(8,128)(2,1)S(1)} %get-tuple-element.7.gg, bf16[224,896]{1,0:T(8,128)(2,1)S(1)} %get-tuple-element.8.gu), custom_call_target="tpu_custom_call" | custom-call | tf_op jit(solution)/shard_map/write_out/pallas_call | solution.py:488

commit v4 on v3

--- a/solution.py
+++ b/solution.py
@@ -86,43 +86,6 @@
     load_up.start()
     load_og.start()
     load_w.start()
-    pl.semaphore_wait(barrier, 7)
-
-    def half(j):
-        return pl.ds(j * DH, DH)
-
-    def ring_copy(unit, j, ssem, dev, own=False):
-        block = panel.at[unit * 2 + core, :, half(j)]
-        return remote(og.at[:, half(j)] if own else block, block, ssem, ring_recv.at[j, unit], dev)
-
-    def go_up(unit, j, own=False):
-        return ring_copy(unit, j, up_send.at[j, unit], z_up, own)
-
-    def go_dn(unit, j, own=False):
-        return ring_copy(unit, j, dn_send.at[j, unit], z_dn, own)
-
-    def to_far(j):
-        return ring_copy(own_unit, j, xh_send.at[j], x_far, True)
-
-    def sib_copy(unit, j, core_, own=False):
-        block = panel.at[unit * 2 + core_, :, half(j)]
-        return remote(
-            og.at[:, half(j)] if own else block, block, sib_send.at[j, unit], sib_recv.at[j, unit], sib
-        )
-
-    def to_sib(unit, j, own=False):
-        return sib_copy(unit, j, core, own)
-
-    for j in range(2):
-        to_far(j).start()
-        go_up(own_unit, j, True).start()
-        go_dn(own_unit, j, True).start()
-    for j in range(2):
-        to_sib(own_unit, j, True).start()
-
-    def hid_copy(c, ssem, dev):
-        return remote(hid.at[c], hid.at[c], ssem, hid_recv.at[c], dev)
-
     load_gate.wait()
     load_up.wait()
 
@@ -136,6 +99,43 @@
         hid[col, rows, :] = (silu * u).astype(BF)
         f_up[rows, :] = silu
         f_gate[rows, :] = u * s * (1.0 + g * (1.0 - s))
+
+    pl.semaphore_wait(barrier, 7)
+
+    def half(j):
+        return pl.ds(j * DH, DH)
+
+    def ring_copy(unit, j, ssem, dev, own=False):
+        block = panel.at[unit * 2 + core, :, half(j)]
+        return remote(og.at[:, half(j)] if own else block, block, ssem, ring_recv.at[j, unit], dev)
+
+    def go_up(unit, j, own=False):
+        return ring_copy(unit, j, up_send.at[j, unit], z_up, own)
+
+    def go_dn(unit, j, own=False):
+        return ring_copy(unit, j, dn_send.at[j, unit], z_dn, own)
+
+    def to_far(j):
+        return ring_copy(own_unit, j, xh_send.at[j], x_far, True)
+
+    def sib_copy(unit, j, core_, own=False):
+        block = panel.at[unit * 2 + core_, :, half(j)]
+        return remote(
+            og.at[:, half(j)] if own else block, block, sib_send.at[j, unit], sib_recv.at[j, unit], sib
+        )
+
+    def to_sib(unit, j, own=False):
+        return sib_copy(unit, j, core, own)
+
+    for j in range(2):
+        to_far(j).start()
+        go_up(own_unit, j, True).start()
+        go_dn(own_unit, j, True).start()
+    for j in range(2):
+        to_sib(own_unit, j, True).start()
+
+    def hid_copy(c, ssem, dev):
+        return remote(hid.at[c], hid.at[c], ssem, hid_recv.at[c], dev)
 
     c_next, c_prev, c_opp = y_next * 2 + xl, y_prev * 2 + xl, y_opp * 2 + xl
     p_own, p_next, p_prev, p_opp = (y_ * 2 + 1 - xl for y_ in (y, y_next, y_prev, y_opp))

time: 77.9 us -> 77.9 us (level)
  no operation moved by 1% of the time
where the time goes in v4:
time: 77.9 us; the launch traced here: 77.8 us
  Pallas kernels  77.2 us (99%)
    pallas_call x1, Pallas kernels, on_device(): pl.pallas_call(kernel, out_shape=(pltpu.VMEM((H, D), BF), pltpu.VMEM((OT,...  75.1 us
    pallas_call x1, Pallas kernels, on_device(): pl.pallas_call(write_out, out_shape=tuple((jax.ShapeDtypeStruct(r.shape,...  2.14 us

profile of v4, /device:TPU:40, one launch (start us, length us, event | category | flops | bytes accessed | tf_op | source)
XLA Modules:
  0.0 77.8 jit_solution(15520955805687968074)
XLA Ops:
  0.6 75.1 %swiglu_down_backward.1 = (bf16[896,2048]{1,0:T(8,128)(2,1)S(1)}, bf16[224,896]{1,0:T(8,128)(2,1)S(1)}, bf16[224,896]{1,0:T(8,128)(2,1)S(1)}) custom-call(bf16[56,2048]{1,0:T(8,128)(2,1)} %og.1, bf16[224,896]{1,0:T(8,128)(2,1)} %gate.1, bf16[224,896]{1,0:T(8,128)(2,1)} %up.1, bf16[896,2048]{1,0:T(8,128)(2,1)} %w_hbm.1), custom_call_target="tpu_custom_call" | custom-call | flops 13153337344 | bytes 9437184 | tf_op jit(solution)/shard_map/swiglu_down_backward/pallas_call | solution.py:453
  75.7 2.1 %write_out.1 = (bf16[896,2048]{1,0:T(8,128)(2,1)}, bf16[224,896]{1,0:T(8,128)(2,1)}, bf16[224,896]{1,0:T(8,128)(2,1)}) custom-call(bf16[896,2048]{1,0:T(8,128)(2,1)S(1)} %get-tuple-element.6.gd, bf16[224,896]{1,0:T(8,128)(2,1)S(1)} %get-tuple-element.7.gg, bf16[224,896]{1,0:T(8,128)(2,1)S(1)} %get-tuple-element.8.gu), custom_call_target="tpu_custom_call" | custom-call | tf_op jit(solution)/shard_map/write_out/pallas_call | solution.py:488

commit v5 on v4

--- a/solution.py
+++ b/solution.py
@@ -33,9 +33,9 @@
     return total
 
 
-MERGED = [0, 0, 2, 3, 5, 7, 9, 11, 11, 14, 16, 16, 16, 16]
-SUMMED = [0, 0, 0, 0, 2, 3, 5, 7, 7, 11, 14, 16, 16, 16]
-FINISHED = [0, 0, 0, 0, 0, 0, 2, 3, 3, 7, 11, 14, 14, 16]
+MERGED = [0, 0, 2, 3, 5, 7, 9, 9, 9, 14, 16, 16, 16, 16]
+SUMMED = [0, 0, 0, 0, 2, 3, 5, 5, 5, 9, 14, 16, 16, 16]
+FINISHED = [0, 0, 0, 0, 0, 0, 2, 2, 2, 5, 9, 14, 14, 16]
 HID_NEAR = 2
 HID_FAR = 4
 

time: 77.9 us -> 78.2 us (level)
  the two profiles are of different devices: /device:TPU:40 before, /device:TPU:6 now
where the time goes in v5:
time: 78.2 us; the launch traced here: 78.1 us
  Pallas kernels  77.5 us (99%)
    pallas_call x1, Pallas kernels, on_device(): pl.pallas_call(kernel, out_shape=(pltpu.VMEM((H, D), BF), pltpu.VMEM((OT,...  75.4 us
    pallas_call x1, Pallas kernels, on_device(): pl.pallas_call(write_out, out_shape=tuple((jax.ShapeDtypeStruct(r.shape,...  2.14 us

profile of v5, /device:TPU:6, one launch (start us, length us, event | category | flops | bytes accessed | tf_op | source)
XLA Modules:
  0.0 78.1 jit_solution(9307895038210201395)
XLA Ops:
  0.6 75.4 %swiglu_down_backward.1 = (bf16[896,2048]{1,0:T(8,128)(2,1)S(1)}, bf16[224,896]{1,0:T(8,128)(2,1)S(1)}, bf16[224,896]{1,0:T(8,128)(2,1)S(1)}) custom-call(bf16[56,2048]{1,0:T(8,128)(2,1)} %og.1, bf16[224,896]{1,0:T(8,128)(2,1)} %gate.1, bf16[224,896]{1,0:T(8,128)(2,1)} %up.1, bf16[896,2048]{1,0:T(8,128)(2,1)} %w_hbm.1), custom_call_target="tpu_custom_call" | custom-call | flops 13153337344 | bytes 9437184 | tf_op jit(solution)/shard_map/swiglu_down_backward/pallas_call | solution.py:453
  76.0 2.1 %write_out.1 = (bf16[896,2048]{1,0:T(8,128)(2,1)}, bf16[224,896]{1,0:T(8,128)(2,1)}, bf16[224,896]{1,0:T(8,128)(2,1)}) custom-call(bf16[896,2048]{1,0:T(8,128)(2,1)S(1)} %get-tuple-element.6.gd, bf16[224,896]{1,0:T(8,128)(2,1)S(1)} %get-tuple-element.7.gg, bf16[224,896]{1,0:T(8,128)(2,1)S(1)} %get-tuple-element.8.gu), custom_call_target="tpu_custom_call" | custom-call | tf_op jit(solution)/shard_map/write_out/pallas_call | solution.py:488
